TPU v7x, 32 devices: a whole 2x2x4 slice. The times are simulated.
32 devices in a mesh: dp: 8 (over y, x, core), mp: 4 (over z).
Axes of the slice: x: 2, y: 2, z: 4, core: 2. Of those that a mesh axis runs over, the one named last changes fastest.
Arguments:
- tokens: bfloat16 [4096, 768], P('dp'), may hold values from -6 to 6
- encoder: bfloat16 [16, 1500, 768], P('dp', 'mp'), may hold values from -6 to 6
- lengths: int32 [8, 2], P('dp'), may hold values from 1 to 448, 512 in all within a row
- norm_gains: float32 [3, 768], replicated, may hold values from 0.5 to 1.5
- norm_biases: float32 [3, 768], replicated, may hold values from -1 to 1
- self_in: bfloat16 [3, 768, 768], P(None, None, 'mp'), may hold values from -0.21875 to 0.21875
- cross_in: bfloat16 [3, 768, 768], P(None, None, 'mp'), may hold values from -0.21875 to 0.21875
- in_biases: float32 [4, 768], P(None, 'mp'), may hold values from -1 to 1
- self_out: bfloat16 [768, 768], P('mp'), may hold values from -0.875 to 0.875
- cross_out: bfloat16 [768, 768], P('mp'), may hold values from -6 to 6
- out_biases: float32 [3, 768], replicated, may hold values from -1 to 1
- fc_up: bfloat16 [768, 3072], P(None, 'mp'), may hold values from -0.21875 to 0.21875
- up_bias: float32 [3072], P('mp'), may hold values from -1 to 1
- fc_down: bfloat16 [3072, 768], P('mp'), may hold values from -0.4375 to 0.4375
- cotangent: bfloat16 [4096, 768], P('dp'), may hold values from -6 to 6
Outputs:
- layer_out: bfloat16 [4096, 768], P('dp')
- token_grad: bfloat16 [4096, 768], P('dp')
- encoder_grad: bfloat16 [16, 1500, 768], P('dp', 'mp')
- norm_gains_grad: float32 [3, 768], replicated
- norm_biases_grad: float32 [3, 768], replicated
- self_in_grad: float32 [3, 768, 768], P(None, 'dp', 'mp')
- cross_in_grad: float32 [3, 768, 768], P(None, 'dp', 'mp')
- in_biases_grad: float32 [4, 768], P(None, 'mp')
- self_out_grad: float32 [768, 768], P('mp', 'dp')
- cross_out_grad: float32 [768, 768], P('mp', 'dp')
- out_biases_grad: float32 [3, 768], replicated
- fc_up_grad: float32 [768, 3072], P('dp', 'mp')
- up_bias_grad: float32 [3072], P('mp')
- fc_down_grad: float32 [3072, 768], P('mp', 'dp')
Inputs may be any that keep to these rules, and one draw needn't show every extreme that they name: `lengths`: each row sums to 512.
All inputs are finite; a program needn't handle non-finite values.
Results may differ from a plain program's by a relative error of at most 0.024.
Values may be sent and summed in bfloat16 or wider, within the bound.
A program may use at most 128 MiB of HBM per device.

v0:
```python
import jax
import jax.numpy as jnp
from jax import lax
from jax.sharding import PartitionSpec as P

HEAD_DIM = 64


epsilon = 1e-05
factor = 0.125
masked_value = -1e30


def layer_norm(values, norm_gain, offset):
    average = jnp.mean(values, axis=-1, keepdims=True)
    centred = values - average
    variance = jnp.mean(centred * centred, axis=-1, keepdims=True)
    return centred * lax.rsqrt(variance + epsilon) * norm_gain + offset


def exact_gelu(values):
    return jax.nn.gelu(values, approximate=False)


def product(left_side, right_side):
    return jnp.dot(left_side, right_side, preferred_element_type=jnp.float32)


def left_product(left_side, right_side):
    return lax.dot_general(
        left_side, right_side, (((0,), (0,)), ((), ())), preferred_element_type=jnp.float32
    )


def right_product(left_side, right_side):
    return lax.dot_general(
        left_side, right_side, (((1,), (1,)), ((), ())), preferred_element_type=jnp.float32
    )


def split_heads(matrix):
    return matrix.reshape(matrix.shape[0], -1, HEAD_DIM).transpose(1, 0, 2)


def merge_heads(stacked):
    return stacked.transpose(1, 0, 2).reshape(stacked.shape[1], -1)


def head_scores(queries, key_rows, allowed):
    return jnp.where(allowed, factor * right_product(queries, key_rows), masked_value)


def attention_forward(queries, key_rows, value_rows, allowed):

    def one_head(inputs):
        scores = head_scores(inputs[0], inputs[1], allowed)
        row_max = jnp.max(scores, axis=-1, keepdims=True)
        exponent = jnp.exp(scores - row_max)
        row_total = jnp.sum(exponent, axis=-1, keepdims=True)
        probabilities = (exponent / row_total).astype(jnp.bfloat16)
        return (product(probabilities, inputs[2]), row_max + jnp.log(row_total))

    outputs, log_totals = lax.map(
        one_head, (split_heads(queries), split_heads(key_rows), split_heads(value_rows))
    )
    return (merge_heads(outputs).astype(jnp.bfloat16), log_totals)


def attention_backward(queries, key_rows, value_rows, allowed, log_totals, upstream):

    def one_head(inputs):
        head_query, head_key, head_value, log_total, head_upstream = inputs
        probabilities = jnp.exp(head_scores(head_query, head_key, allowed) - log_total)
        value_grad = left_product(probabilities.astype(jnp.bfloat16), head_upstream)
        prob_grad = right_product(head_upstream, head_value)
        row_inner = jnp.sum(probabilities * prob_grad, axis=-1, keepdims=True)
        score_grad = (probabilities * (prob_grad - row_inner)).astype(jnp.bfloat16)
        return (
            factor * product(score_grad, head_key),
            factor * left_product(score_grad, head_query),
            value_grad,
        )

    query_grad, key_grad, value_grad = lax.map(
        one_head,
        (
            split_heads(queries),
            split_heads(key_rows),
            split_heads(value_rows),
            log_totals,
            split_heads(upstream),
        ),
    )
    return (merge_heads(query_grad), merge_heads(key_grad), merge_heads(value_grad))


def shards(
    tokens,
    encoder,
    lengths,
    norm_gains,
    norm_biases,
    self_in,
    cross_in,
    in_biases,
    self_out,
    cross_out,
    out_biases,
    fc_up,
    up_bias,
    fc_down,
    cotangent,
):
    bf16 = jnp.bfloat16
    row_count = tokens.shape[0]
    clip_count = encoder.shape[0]
    positions = jnp.arange(row_count, dtype=jnp.int32)
    clip_ends = jnp.cumsum(lengths[0])
    token_clip = jnp.sum((positions[:, None] >= clip_ends[None, :]).astype(jnp.int32), axis=1)
    self_allowed = (token_clip[:, None] == token_clip[None, :]) & (
        positions[None, :] <= positions[:, None]
    )
    frame_piece = lax.all_gather(encoder, "mp", axis=1, tiled=True)
    key_piece = jnp.einsum(
        "cfd,de->cfe", frame_piece, cross_in[1], preferred_element_type=jnp.float32
    )
    value_piece = (
        jnp.einsum("cfd,de->cfe", frame_piece, cross_in[2], preferred_element_type=jnp.float32)
        + in_biases[3]
    )
    cross_keys = key_piece.astype(bf16)
    cross_values = value_piece.astype(bf16)
    frames = frame_piece
    frame_count = frames.shape[1]
    frames = frames.reshape(clip_count * frame_count, -1)
    cross_keys = cross_keys.reshape(clip_count * frame_count, -1)
    cross_values = cross_values.reshape(clip_count * frame_count, -1)
    frame_clip = jnp.arange(clip_count * frame_count, dtype=jnp.int32) // frame_count
    cross_allowed = token_clip[:, None] == frame_clip[None, :]
    inputs = tokens.astype(jnp.float32)
    normed_self, pull_first = jax.vjp(layer_norm, inputs, norm_gains[0], norm_biases[0])
    normed_self = normed_self.astype(bf16)
    self_queries = (product(normed_self, self_in[0]) + in_biases[0]).astype(bf16)
    self_keys = product(normed_self, self_in[1]).astype(bf16)
    self_values = (product(normed_self, self_in[2]) + in_biases[1]).astype(bf16)
    self_attended, self_totals = attention_forward(
        self_queries, self_keys, self_values, self_allowed
    )
    middle = inputs + lax.psum(product(self_attended, self_out), "mp") + out_biases[0]
    normed_cross, pull_second = jax.vjp(layer_norm, middle, norm_gains[1], norm_biases[1])
    normed_cross = normed_cross.astype(bf16)
    cross_queries = (product(normed_cross, cross_in[0]) + in_biases[2]).astype(bf16)
    cross_attended, cross_totals = attention_forward(
        cross_queries, cross_keys, cross_values, cross_allowed
    )
    after_cross = middle + lax.psum(product(cross_attended, cross_out), "mp") + out_biases[1]
    normed_mlp, pull_third = jax.vjp(layer_norm, after_cross, norm_gains[2], norm_biases[2])
    normed_mlp = normed_mlp.astype(bf16)
    upward = product(normed_mlp, fc_up) + up_bias
    active, pull_gelu = jax.vjp(exact_gelu, upward)
    active = active.astype(bf16)
    layer_out = (after_cross + lax.psum(product(active, fc_down), "mp") + out_biases[2]).astype(
        bf16
    )
    grad_out = cotangent.astype(jnp.float32)
    down_bias_grad = jnp.sum(grad_out, axis=0)
    grad_low = grad_out.astype(bf16)
    fc_down_grad = left_product(active, grad_low)
    (upward_grad,) = pull_gelu(right_product(grad_low, fc_down))
    up_bias_grad = jnp.sum(upward_grad, axis=0)
    upward_low = upward_grad.astype(bf16)
    fc_up_grad = left_product(normed_mlp, upward_low)
    mlp_normed_grad = lax.psum(right_product(upward_low, fc_up), "mp")
    cross_side_grad, third_gain_grad, third_bias_grad = pull_third(mlp_normed_grad)
    cross_side_grad = cross_side_grad + grad_out
    cross_bias_grad = jnp.sum(cross_side_grad, axis=0)
    cross_side_low = cross_side_grad.astype(bf16)
    cross_out_grad = left_product(cross_attended, cross_side_low)
    cross_upstream = right_product(cross_side_low, cross_out).astype(bf16)
    cross_query_grad, cross_key_grad, cross_value_grad = attention_backward(
        cross_queries, cross_keys, cross_values, cross_allowed, cross_totals, cross_upstream
    )
    cross_query_bias = jnp.sum(cross_query_grad, axis=0)
    cross_value_bias = jnp.sum(cross_value_grad, axis=0)
    cross_query_low = cross_query_grad.astype(bf16)
    cross_key_low = cross_key_grad.astype(bf16)
    cross_value_low = cross_value_grad.astype(bf16)
    cross_normed_grad = lax.psum(right_product(cross_query_low, cross_in[0]), "mp")
    cross_in_grad = jnp.stack(
        [
            left_product(normed_cross, cross_query_low),
            left_product(frames, cross_key_low),
            left_product(frames, cross_value_low),
        ]
    )
    frame_term = right_product(cross_key_low, cross_in[1]) + right_product(
        cross_value_low, cross_in[2]
    )
    encoder_grad = lax.psum_scatter(
        frame_term.reshape(clip_count, frame_count, -1), "mp", scatter_dimension=1, tiled=True
    ).astype(bf16)
    middle_grad, second_gain_grad, second_bias_grad = pull_second(cross_normed_grad)
    middle_grad = middle_grad + cross_side_grad
    self_bias_grad = jnp.sum(middle_grad, axis=0)
    middle_low = middle_grad.astype(bf16)
    self_out_grad = left_product(self_attended, middle_low)
    self_upstream = right_product(middle_low, self_out).astype(bf16)
    self_query_grad, self_key_grad, self_value_grad = attention_backward(
        self_queries, self_keys, self_values, self_allowed, self_totals, self_upstream
    )
    self_query_bias = jnp.sum(self_query_grad, axis=0)
    self_value_bias = jnp.sum(self_value_grad, axis=0)
    self_query_low = self_query_grad.astype(bf16)
    self_key_low = self_key_grad.astype(bf16)
    self_value_low = self_value_grad.astype(bf16)
    self_in_grad = jnp.stack(
        [
            left_product(normed_self, self_query_low),
            left_product(normed_self, self_key_low),
            left_product(normed_self, self_value_low),
        ]
    )
    self_term = (
        right_product(self_query_low, self_in[0])
        + right_product(self_key_low, self_in[1])
        + right_product(self_value_low, self_in[2])
    )
    self_normed_grad = lax.psum(self_term, "mp")
    input_grad, first_gain_grad, first_bias_grad = pull_first(self_normed_grad)
    token_grad = (input_grad + middle_grad).astype(bf16)
    norm_gains_grad = jnp.stack([first_gain_grad, second_gain_grad, third_gain_grad])
    norm_biases_grad = jnp.stack([first_bias_grad, second_bias_grad, third_bias_grad])
    in_biases_grad = jnp.stack(
        [self_query_bias, self_value_bias, cross_query_bias, cross_value_bias]
    )
    out_biases_grad = jnp.stack([self_bias_grad, cross_bias_grad, down_bias_grad])
    self_in_grad, cross_in_grad, self_out_grad, cross_out_grad, fc_up_grad, fc_down_grad = (
        lax.psum_scatter(self_in_grad, "dp", scatter_dimension=1, tiled=True),
        lax.psum_scatter(cross_in_grad, "dp", scatter_dimension=1, tiled=True),
        lax.psum_scatter(self_out_grad, "dp", scatter_dimension=1, tiled=True),
        lax.psum_scatter(cross_out_grad, "dp", scatter_dimension=1, tiled=True),
        lax.psum_scatter(fc_up_grad, "dp", scatter_dimension=0, tiled=True),
        lax.psum_scatter(fc_down_grad, "dp", scatter_dimension=1, tiled=True),
    )
    norm_gains_grad, norm_biases_grad, in_biases_grad, out_biases_grad, up_bias_grad = lax.psum(
        (norm_gains_grad, norm_biases_grad, in_biases_grad, out_biases_grad, up_bias_grad), "dp"
    )
    return (
        layer_out,
        token_grad,
        encoder_grad,
        norm_gains_grad,
        norm_biases_grad,
        self_in_grad,
        cross_in_grad,
        in_biases_grad,
        self_out_grad,
        cross_out_grad,
        out_biases_grad,
        fc_up_grad,
        up_bias_grad,
        fc_down_grad,
    )


def solution(mesh):
    in_specs = (
        P("dp", None),
        P("dp", "mp", None),
        P("dp", None),
        P(),
        P(),
        P(None, None, "mp"),
        P(None, None, "mp"),
        P(None, "mp"),
        P("mp", None),
        P("mp", None),
        P(),
        P(None, "mp"),
        P("mp"),
        P("mp", None),
        P("dp", None),
    )
    out_specs = (
        P("dp", None),
        P("dp", None),
        P("dp", "mp", None),
        P(),
        P(),
        P(None, "dp", "mp"),
        P(None, "dp", "mp"),
        P(None, "mp"),
        P("mp", "dp"),
        P("mp", "dp"),
        P(),
        P("dp", "mp"),
        P("mp"),
        P("mp", "dp"),
    )
    return jax.shard_map(shards, mesh=mesh, in_specs=in_specs, out_specs=out_specs, check_vma=False)
```

profile of v0, /device:TPU:0, one launch (start us, length us, event | category | flops | bytes accessed | tf_op | source)
XLA Modules:
  0.0 1117.9 jit_solution(663117936983168179)
XLA Ops:
  16.5 2.8 while.56
  19.4 2.7 fusion.170
  23.7 70.5 %all-reduce.10.cloned.1.call-done = f32[512,768]{1,0:T(8,128)} async-done(((f32[512,768]{1,0:T(8,128)}), f32[512,768]{1,0:T(8,128)}) %all-reduce.10.cloned.1.call-update) | async-done | bytes 1572880 | tf_op jit(solution)/shard_map/psum | solution.py:149
  98.8 83.6 %all-gather.2.cloned.1.call-done = bf16[2,1500,768]{2,0,1:T(2,128)(2,1)} async-done(((bf16[2,375,768]{2,0,1:T(2,128)(2,1)}), bf16[2,1500,768]{2,0,1:T(2,128)(2,1)}) %all-gather.2.cloned.1.call-update) | async-done | bytes 4608016 | tf_op jit(solution)/shard_map/all_gather | solution.py:123
  182.4 3.9 fusion.88
  188.5 4.8 reshape_reshape.9
  193.3 3.7 copy.82
  197.0 3.9 convolution_convert_fusion
  203.1 4.3 reshape_reshape.8
  207.4 3.7 copy.81
  211.2 18.9 %while.57 = (s32[]{:T(128)}, bf16[3,512,64]{1,2,0:T(8,128)(2,1)S(1)}, f32[3,512,1]{1,2,0:T(1,128)S(1)}, bf16[3,512,64]{2,1,0:T(8,128)(2,1)S(1)}, bf16[3,3000,64]...) while((s32[]{:T(128)}, ...), condition=%wide.region_14.15_spmd.clone, body=%wide.region_11.14_spmd.clone.sunk | while | flops 407039488 | bytes 20267112 | solution.py:63
  211.2 3.1 fusion.255
  217.5 3.1 fusion.255
  223.8 3.1 fusion.255
  230.1 2.7 fusion.171
  233.0 67.6 %all-reduce.12.cloned.1.call-done = f32[512,768]{1,0:T(8,128)} async-done(((f32[512,768]{1,0:T(8,128)}), f32[512,768]{1,0:T(8,128)}) %all-reduce.12.cloned.1.call-update) | async-done | bytes 1572880 | tf_op jit(solution)/shard_map/psum | solution.py:156
  305.3 5.9 fusion.158
  314.2 68.2 %all-reduce.14.cloned.1.call-done = f32[512,768]{1,0:T(8,128)} async-done(((f32[512,768]{1,0:T(8,128)}), f32[512,768]{1,0:T(8,128)}) %all-reduce.14.cloned.1.call-update) | async-done | bytes 1572880 | tf_op jit(solution)/shard_map/psum | solution.py:173
  382.4 3.2 multiply_reduce_fusion.2
  391.5 46.9 %while.58 = (s32[]{:T(128)}, f32[3,512,64]{1,2,0:T(8,128)}, bf16[3,3000,64]{1,2,0:T(8,128)(2,1)}, f32[3,3000,64]{1,2,0:T(8,128)}, bf16[3,512,64]{2,1,0:T(8,128)(...) while((s32[]{:T(128)}, f32[3,512,64]{1,2,0:T(8,128)}, ...), condition=%wide.region_24.25_spmd.clone, body=%wide.region_22.24_spmd.clone.sunk | while | flops 998624256 | bytes 60644564 | solution.py:84
  394.4 3.6 multiply_reduce_fusion.10
  399.7 2.8 fusion.269
  410.0 3.6 multiply_reduce_fusion.10
  415.3 2.8 fusion.269
  425.6 3.6 multiply_reduce_fusion.10
  430.9 2.9 fusion.269
  433.8 2.5 fusion.267
  442.6 5.0 copy.77
  447.6 5.3 reshape.292
  457.9 2.9 bitcast_convert_fusion
  461.1 49.8 %all-reduce.16.cloned.1.call-done = f32[512,768]{1,0:T(8,128)} async-done(((f32[512,768]{1,0:T(8,128)}), f32[512,768]{1,0:T(8,128)}) %all-reduce.16.cloned.1.call-update) | async-done | bytes 1572880 | tf_op jit(solution)/shard_map/psum | solution.py:188
  510.9 2.7 multiply_reduce_fusion.3
  518.2 3.9 convolution_bitcast_fusion.5
  522.2 3.6 convolution_bitcast_fusion.6
  527.1 4.2 copy.93
  531.4 4.7 reshape.297
  541.0 23.0 %while.59 = (s32[]{:T(128)}, f32[3,512,64]{1,2,0:T(8,128)}, bf16[3,512,64]{1,2,0:T(8,128)(2,1)}, f32[3,512,64]{1,2,0:T(8,128)}, bf16[3,512,64]{2,1,0:T(8,128)(2,...) while((s32[]{:T(128)}, f32[3,512,64]{1,2,0:T(8,128)}, ...), condition=%wide.region_30.31_spmd.clone, body=%wide.region_28.30_spmd.clone.sunk | while | flops 170982912 | bytes 10767537 | solution.py:84
  568.1 4.2 copy.91
  572.3 4.7 reshape.295
  588.3 3.5 fusion.114
  591.9 2.9 fusion.121
  594.7 6.1 convolution_add_fusion
  600.8 8.3 reshape.285
  609.1 27.3 %copy.87 = f32[2,1500,768]{2,0,1:T(2,128)} copy(f32[2,1500,768]{2,1,0:T(8,128)} %reshape.285) | data formatting | bytes 18432000 | tf_op jit(solution)/shard_map/reshape | solution.py:200
  636.5 412.1 %all-reduce.19 = bf16[2,1500,768]{2,0,1:T(2,128)(2,1)} all-reduce(f32[2,1500,768]{2,0,1:T(2,128)} %copy.87), channel_id=2, replica_groups=mesh['dp'=8,'mp'=4] {'mp'}, use_global_device_ids=true, to_apply=%region_34.35.clone | all-reduce | flops 2304000 | bytes 13824000
  1055.6 3.1 dynamic-slice_convert_fusion
  1082.1 23.9 %all-reduce.1 = (f32[3,768]{1,0:T(4,128)}, f32[3,768]{1,0:T(4,128)}, f32[4,192]{1,0:T(4,128)}, f32[3,768]{1,0:T(4,128)}, f32[768]{0:T(1024)}) all-reduce(f32[3,768]{1,0:T(4,128)} %pad_maximum_fusion.2, f32[3,768]{1,0:T(4,128)} %pad_maximum_fusion.3, f32[4,192]{1,0:T(4,128)} %pad_maximum_fusion.5, ...), channel_id=1, replica_groups=mesh['dp'=8,'mp'=4] {'dp'}, use_global_device_ids=true, to_apply=%region_38.39 | all-reduce | flops 8448 | bytes 67584 | tf_op jit(solution)/shard_map/psum | solution.py:245
  1106.7 2.6 add_convert_fusion.1
  (423 shorter events, 160.3 us)
Async XLA Ops:
  7.2 297.9 %copy-start = (bf16[768,768]{1,0:T(8,128)(2,1)S(1)}, bf16[768,768]{1,0:T(8,128)(2,1)}, u32[]{:S(2)}) copy-start(bf16[768,768]{1,0:T(8,128)(2,1)} %param.36) | copy-start | bytes 3538948
  7.2 5.3 copy-start.4
  7.2 4.1 copy-start.95
  7.2 4.7 copy-start.92
  7.2 4.7 copy-start.93
  7.2 86.9 %all-reduce.10.cloned.1.call-start = ((), (), s32[]{:S(2)}) async-start(), calls=%async_computation.6 | async-start | bytes 3145728 | tf_op jit(solution)/shard_map/psum | solution.py:149
  7.3 5.6 copy-start.21
  9.7 3.7 copy-start.52
  22.2 160.2 %all-gather.2.cloned.1.call-start = ((), (), s32[]{:S(2)}) async-start(), calls=%async_computation.7 | async-start | bytes 5760000 | tf_op jit(solution)/shard_map/all_gather | solution.py:123
  23.0 277.6 %all-reduce.12.cloned.1.call-start = ((), (), s32[]{:S(2)}) async-start(), calls=%async_computation.8 | async-start | bytes 3145728 | tf_op jit(solution)/shard_map/psum | solution.py:156
  96.9 85.5 %copy-start.98 = (f32[1,192]{1,0:T(1,128)S(1)}, f32[1,192]{1,0:T(1,128)}, u32[]{:S(2)}) copy-start(f32[1,192]{1,0:T(1,128)} %get-tuple-element.533) | copy-start | bytes 2308
  207.4 3.8 copy-start.29
  230.1 70.5 %copy-start.84 = (f32[768]{0:T(1024)S(1)}, f32[768]{0:T(1024)}, u32[]{:S(2)}) copy-start(f32[768]{0:T(1024)} %get-tuple-element.421) | copy-start | bytes 9220
  232.9 149.5 %all-reduce.14.cloned.1.call-start = ((), (), s32[]{:S(2)}) async-start(), calls=%async_computation.9 | async-start | bytes 3145728 | tf_op jit(solution)/shard_map/psum | solution.py:173
  305.3 5.9 copy-start.46
  314.1 196.8 %all-reduce.16.cloned.1.call-start = ((), (), s32[]{:S(2)}) async-start(), calls=%async_computation.10 | async-start | bytes 3145728 | tf_op jit(solution)/shard_map/psum | solution.py:188
  382.4 3.3 copy-start.20
  382.4 3.3 copy-start.61
  382.4 3.3 copy-start.66
  382.4 3.3 copy-start.78
  442.6 616.0 %reduce-scatter.25.cloned.1.call-start = ((), (), s32[]{:S(2)}) async-start(), calls=%async_computation.16 | async-start | bytes 884736
  447.6 7.9 copy-start.71
  457.9 53.0 %copy-start.55 = (f32[768]{0:T(1024)S(1)}, f32[768]{0:T(1024)}, u32[]{:S(2)}) copy-start(f32[768]{0:T(1024)} %get-tuple-element.537) | copy-start | bytes 9220
  457.9 53.0 %copy-start.57 = (f32[512]{0:T(512)S(1)}, f32[512]{0:T(512)}, u32[]{:S(2)}) copy-start(f32[512]{0:T(512)} %copy-done.56) | copy-start | bytes 6148
  457.9 53.0 %copy-start.69 = (f32[512]{0:T(512)S(1)}, f32[512]{0:T(512)}, u32[]{:S(2)}) copy-start(f32[512]{0:T(512)} %copy-done.68) | copy-start | bytes 6148
  460.8 607.0 %reduce-scatter.23.cloned.1.call-start = ((), (), s32[]{:S(2)}) async-start(), calls=%async_computation.15 | async-start | bytes 884736
  510.9 3.4 copy-start.19
  516.8 19.4 %copy-start.6 = (f32[512,768]{1,0:T(8,128)}, f32[512,768]{1,0:T(8,128)S(1)}, u32[]{:S(2)}) copy-start(f32[512,768]{1,0:T(8,128)S(1)} %get-tuple-element.529) | copy-start | bytes 4718596
  518.2 551.2 %reduce-scatter.21.cloned.1.call-start = ((), (), s32[]{:S(2)}) async-start(), calls=%async_computation.14 | async-start | bytes 2211840
  518.2 4.0 copy-start.40
  522.2 3.6 copy-start.37
  536.1 537.0 %reduce-scatter.19.cloned.1.call-start = ((), (), s32[]{:S(2)}) async-start(), calls=%async_computation.13 | async-start | bytes 2211840
  541.0 24.1 %copy-start.14 = (bf16[512,768]{1,0:T(8,128)(2,1)S(1)}, bf16[512,768]{1,0:T(8,128)(2,1)}, u32[]{:S(2)}) copy-start(bf16[512,768]{1,0:T(8,128)(2,1)} %copy-done.13) | copy-start | bytes 2359300
  577.0 499.7 %all-reduce.18.cloned.1.call-start = ((), (), s32[]{:S(2)}) async-start(), calls=%async_computation.17 | async-start | bytes 6291456 | tf_op jit(solution)/shard_map/psum | solution.py:162
  584.1 526.7 %reduce-scatter.17.cloned.1.call-start = ((), (), s32[]{:S(2)}) async-start(), calls=%async_computation.12 | async-start | bytes 2654208 | tf_op jit(solution)/shard_map/reduce_scatter | solution.py:243
  586.4 524.4 %reduce-scatter.15.cloned.1.call-start = ((), (), s32[]{:S(2)}) async-start(), calls=%async_computation.11 | async-start | bytes 2654208 | tf_op jit(solution)/shard_map/reduce_scatter | solution.py:242
  636.5 412.1 %copy-start.81 = (f32[768]{0:T(1024)S(1)}, f32[768]{0:T(1024)}, u32[]{:S(2)}) copy-start(f32[768]{0:T(1024)} %get-tuple-element.409) | copy-start | bytes 9220
  636.5 412.7 %copy-start.80 = (f32[768]{0:T(1024)S(1)}, f32[768]{0:T(1024)}, u32[]{:S(2)}) copy-start(f32[768]{0:T(1024)} %get-tuple-element.416) | copy-start | bytes 9220
  1048.5 5.0 copy-start.32
  1052.2 8.1 copy-start.83
  1052.2 9.3 copy-start.86
  1052.2 9.9 copy-start.82
  1052.2 10.4 copy-start.31
  1054.2 6.6 copy-start.87
  1063.4 13.3 %copy-start.5 = (bf16[512,768]{1,0:T(8,128)(2,1)S(1)}, bf16[512,768]{1,0:T(8,128)(2,1)}, u32[]{:S(2)}) copy-start(bf16[512,768]{1,0:T(8,128)(2,1)} %param.23) | copy-start | bytes 2359300
  1063.4 13.3 %copy-start.51 = (f32[768]{0:T(1024)S(1)}, f32[768]{0:T(1024)}, u32[]{:S(2)}) copy-start(f32[768]{0:T(1024)} %copy-done.50) | copy-start | bytes 9220
  1063.4 13.3 %copy-start.53 = (f32[512]{0:T(512)S(1)}, f32[512]{0:T(512)}, u32[]{:S(2)}) copy-start(f32[512]{0:T(512)} %copy-done.52) | copy-start | bytes 6148
  1074.9 4.5 copy-start.64
  (78 other events, 146.2 us)
Sparse Core Ops, SparseCore 0:
  22.3 71.8 all-reduce.9
  95.7 86.6 all-gather.1
  233.0 67.5 all-reduce.11
  314.2 68.1 all-reduce.13
  442.7 68.1 all-reduce.15
  513.9 34.0 reduce-scatter.24
  551.7 35.0 reduce-scatter.22
  590.2 40.3 reduce-scatter.20
  634.3 40.2 reduce-scatter.18
  676.9 220.8 all-reduce.17
  901.7 42.6 reduce-scatter.16
  948.6 42.4 reduce-scatter.14
where the time goes:
time: 1130 us; the launch traced here: 1120 us
  blocking collectives  436 us (39%)
  waiting for transfers between devices  341 us (30%)
  matrix products  140 us (12%)
  local copies, waits for them, and re-layouts  130 us (12%)
  other arithmetic  53.6 us (5%)
  between operations  16.2 us (1%)
    unnamed x1, blocking collectives  412 us
    all_gather x1, waiting for transfers between devices, shards(): frame_piece = lax.all_gather(encoder, 'mp', axis=1, tiled=True)  83.6 us
    psum x1, waiting for transfers between devices, shards(): lax.psum(product(self_attended, self_out), 'mp')  70.5 us
    psum x1, waiting for transfers between devices, shards(): mlp_normed_grad = lax.psum(right_product(upward_low, fc_up), 'mp')  68.2 us
    psum x1, waiting for transfers between devices, shards(): lax.psum(product(cross_attended, cross_out), 'mp')  67.6 us
    dot_general x28, matrix products, right_product(): lax.dot_general(left_side, right_side, (((1,), (1,)), ((), ())), preferre...  60.8 us
    psum x1, waiting for transfers between devices, shards(): lax.psum(right_product(cross_query_low, cross_in[0]), 'mp')  49.8 us
    unnamed x211, local copies, waits for them, and re-layouts  43.5 us
  transfers between devices with their start and end apart: 12, of which 5 were waited for; matrix products, arithmetic and copies ran while one was open for 16% of the time, Pallas kernels for 0%

commit v1 on v0

v1 whole, which is shorter than its diff:
```python
import functools

import jax
import jax.numpy as jnp
from jax import lax
from jax.experimental import pallas as pl
from jax.experimental.pallas import tpu as pltpu
from jax.sharding import PartitionSpec as P

HEAD_DIM = 64
epsilon = 1e-05
factor = 0.125
masked_value = -1e30
f32 = jnp.float32
bf16 = jnp.bfloat16
MESH = pl.DeviceIdType.MESH
VMEM = pl.BlockSpec(memory_space=pltpu.VMEM)
ANY = pl.BlockSpec(memory_space=pl.ANY)
PLANE = 8


def flip(index, bit):
    return index + bit - 2 * bit * lax.rem(index // bit, 2)


def remote(src, dst, send, recv, device):
    return pltpu.make_async_remote_copy(
        src_ref=src, dst_ref=dst, send_sem=send, recv_sem=recv, device_id=device, device_id_type=MESH
    )


def greet(devices):
    barrier = pltpu.get_barrier_semaphore()
    for device in devices:
        pl.semaphore_signal(barrier, inc=1, device_id=device, device_id_type=MESH)


def pair_sum(left, right):
    return (left.astype(f32) + right.astype(f32)).astype(bf16)


def gather_kernel(pack, attended, weights, parts, own, zsend, wsend, wrecv, osend, orecv, local):
    d, m = lax.axis_index("dp"), lax.axis_index("mp")
    mine = lax.rem(d, PLANE)
    base = d - mine
    up, down = m < 3, m > 0
    barrier = pltpu.get_barrier_semaphore()
    greet([(base + flip(mine, 1), m), (base + flip(mine, 2), m), (base + flip(mine, 4), m)])
    greet([(base + flip(flip(mine, 2), 4), m)])

    @pl.when(up)
    def _():
        greet([(d, m + 1)])

    @pl.when(down)
    def _():
        greet([(d, m - 1)])

    both = jnp.logical_and(up, down)

    @pl.when(both)
    def _():
        pl.semaphore_wait(barrier, 6)

    @pl.when(jnp.logical_not(both))
    def _():
        pl.semaphore_wait(barrier, 5)

    def weight_hop(k, step):
        o = m - step * k
        src = pack.at[mine] if k == 0 else weights.at[o, mine]
        return remote(src, weights.at[o, mine], zsend.at[k, (step + 1) // 2], wrecv.at[o, mine], (d, m + step))

    def part_hop(k, step):
        o = m - step * k
        src = attended if k == 0 else parts.at[o]
        return remote(src, parts.at[o], osend.at[k, (step + 1) // 2], orecv.at[o], (d, m + step))

    def weight_came(o, s):
        remote(weights.at[o, s], weights.at[o, s], wsend.at[0, 0], wrecv.at[o, s], (d, m)).wait_recv()

    def spread(o, k):
        to = base + (flip(mine, k) if k != 6 else flip(flip(mine, 2), 4))
        return remote(weights.at[o, mine], weights.at[o, mine], wsend.at[o, k], wrecv.at[o, mine], (to, m))

    def pass_on(o, k):
        s = flip(mine, k) if k != 6 else flip(flip(mine, 2), 4)
        to = base + flip(mine, 1)
        return remote(weights.at[o, s], weights.at[o, s], wsend.at[o, k + 1], wrecv.at[o, s], (to, m))

    whole = pltpu.make_async_copy(pack, weights.at[m], local.at[0])
    whole.start()
    own_part = pltpu.make_async_copy(attended, parts.at[m], local.at[1])
    own_part.start()
    steps = ((1, up), (-1, down))
    for hop in (weight_hop, part_hop):
        for step, can in steps:

            @pl.when(can)
            def _(hop=hop, step=step):
                hop(0, step).start()

    def origin(k, step):
        o = m - step * k
        return o, (o >= 0) if step > 0 else (o <= 3)

    for k in (1, 2, 3):
        for step, can in steps:
            o, have = origin(k, step)

            @pl.when(have)
            def _(o=o, k=k, step=step, can=can):
                weight_came(o, mine)
                if k < 3:

                    @pl.when(can)
                    def _():
                        weight_hop(k, step).start()

                for way in (6, 2, 4, 1):
                    spread(o, way).start()

    for k in (1, 2, 3):
        for step, can in steps:
            o, have = origin(k, step)

            @pl.when(have)
            def _(o=o, k=k, step=step, can=can):
                remote(parts.at[o], parts.at[o], osend.at[0, 0], orecv.at[o], (d, m)).wait_recv()
                if k < 3:

                    @pl.when(can)
                    def _():
                        part_hop(k, step).start()

    for k in (1, 2, 3):
        for step, can in steps:
            o, have = origin(k, step)

            @pl.when(have)
            def _(o=o):
                for way in (2, 4, 6):
                    s = flip(mine, way) if way != 6 else flip(flip(mine, 2), 4)
                    weight_came(o, s)
                    pass_on(o, way).start()

    for j in (1, 2, 3):
        o = lax.rem(m + j, 4)
        for way in (0, 2, 4, 6):
            s = flip(mine, way) if way in (2, 4) else (mine if way == 0 else flip(flip(mine, 2), 4))
            weight_came(o, flip(s, 1))
    for k in (0, 1, 2):
        for step, can in steps:
            o, have = origin(k, step)

            @pl.when(jnp.logical_and(have, can))
            def _(k=k, step=step):
                weight_hop(k, step).wait_send()
                part_hop(k, step).wait_send()

    for j in (1, 2, 3):
        o = lax.rem(m + j, 4)
        for way in (1, 2, 4, 6):
            spread(o, way).wait_send()
        for way in (2, 4, 6):
            pass_on(o, way).wait_send()
    whole.wait()
    own_part.wait()
    own[...] = jnp.zeros_like(own)


def gather(pack, attended):
    rows, cols = pack.shape[1:]
    dma = pltpu.SemaphoreType.DMA
    weights, parts, _ = pl.pallas_call(
        gather_kernel,
        out_shape=(
            jax.ShapeDtypeStruct((4,) + pack.shape, bf16),
            jax.ShapeDtypeStruct((4,) + attended.shape, bf16),
            jax.ShapeDtypeStruct((8, 128), f32),
        ),
        in_specs=[ANY, ANY],
        out_specs=[ANY, ANY, VMEM],
        scratch_shapes=[
            dma((3, 2)), dma((4, 8)), dma((4, 8)), dma((3, 2)), dma((4,)), dma((2,)),
        ],
        compiler_params=pltpu.CompilerParams(collective_id=1, has_side_effects=True),
        name="gather",
    )(pack, attended)
    return weights, parts


def total_kernel(count, lag, x_ref, o_ref, from_edge, half, other, whole, sa, ra, sb, rb, sr, rr):
    d, m = lax.axis_index("dp"), lax.axis_index("mp")
    edge = jnp.logical_or(m == 0, m == 3)
    inner = jnp.logical_not(edge)
    near, peer = flip(m, 1), 3 - m
    barrier = pltpu.get_barrier_semaphore()
    greet([(d, near)])

    @pl.when(inner)
    def _():
        greet([(d, peer)])
        pl.semaphore_wait(barrier, 2)

    @pl.when(edge)
    def _():
        pl.semaphore_wait(barrier, 1)

    rows = x_ref.shape[0] // count

    def block(c):
        return pl.ds(c * rows, rows)

    def inward(c):
        return remote(x_ref.at[block(c)], from_edge.at[c], sa.at[c], ra.at[c], (d, near))

    def across(c):
        return remote(half.at[c], other.at[c], sb.at[c], rb.at[c], (d, peer))

    def outward(c):
        return remote(whole.at[c], whole.at[c], sr.at[c], rr.at[c], (d, near))

    @pl.when(edge)
    def _():
        for c in range(count):
            inward(c).start()
        for c in range(count):
            outward(c).wait_recv()
            o_ref[block(c)] = whole[c]
        for c in range(count):
            inward(c).wait_send()

    @pl.when(inner)
    def _():
        for i in range(count + lag):
            if i < count:
                inward(i).wait_recv()
                half[i] = pair_sum(x_ref[block(i)], from_edge[i])
                across(i).start()
            c = i - lag
            if c >= 0:
                across(c).wait_recv()
                value = pair_sum(half[c], other[c])
                whole[c] = value
                outward(c).start()
                o_ref[block(c)] = value
        for c in range(count):
            across(c).wait_send()
            outward(c).wait_send()


def total(x, count=16, lag=3):
    rows, cols = x.shape
    buffer = pltpu.VMEM((count, rows // count, cols), bf16)
    dma = pltpu.SemaphoreType.DMA((count,))
    return pl.pallas_call(
        functools.partial(total_kernel, count, lag),
        out_shape=jax.ShapeDtypeStruct(x.shape, bf16),
        in_specs=[VMEM],
        out_specs=VMEM,
        scratch_shapes=[buffer] * 4 + [dma] * 6,
        compiler_params=pltpu.CompilerParams(collective_id=2, has_side_effects=True),
        name="total",
    )(x)


def share_kernel(x_ref, o_ref, slots, send, recv):
    d, m = lax.axis_index("dp"), lax.axis_index("mp")
    greet([(d, lax.rem(m + k, 4)) for k in (1, 2, 3)])
    pl.semaphore_wait(pltpu.get_barrier_semaphore(), 3)
    for k in (1, 2, 3):
        remote(x_ref, slots.at[m], send.at[k], recv.at[m], (d, lax.rem(m + k, 4))).start()
    slots[m] = x_ref[...]
    for k in (1, 2, 3):
        o = lax.rem(m + k, 4)
        remote(x_ref, slots.at[o], send.at[k], recv.at[o], (d, o)).wait_recv()
    o_ref[...] = slots[...]
    for k in (1, 2, 3):
        remote(x_ref, slots.at[m], send.at[k], recv.at[m], (d, lax.rem(m + k, 4))).wait_send()


def share(x, number):
    return pl.pallas_call(
        share_kernel,
        out_shape=jax.ShapeDtypeStruct((4,) + x.shape, x.dtype),
        in_specs=[VMEM],
        out_specs=VMEM,
        scratch_shapes=[
            pltpu.VMEM((4,) + x.shape, x.dtype), pltpu.SemaphoreType.DMA((4,)), pltpu.SemaphoreType.DMA((4,)),
        ],
        compiler_params=pltpu.CompilerParams(collective_id=number, has_side_effects=True),
        name="share",
    )(x)


def scatter_kernel(n, x_ref, o_ref, z_ref, came, half, slots, mine, blocks, s1, r1, s2, r2, s3, r3):
    d, m = lax.axis_index("dp"), lax.axis_index("mp")
    core, chip = lax.rem(d, 2), d // 2
    chips = n // 2
    sibling = flip(d, 1)
    greet([(sibling, m)])
    for k in range(1, chips):
        greet([(2 * lax.rem(chip + k, chips) + core, m)])
    for k in (1, 2, 3):
        greet([(d, lax.rem(m + k, 4))])
    pl.semaphore_wait(pltpu.get_barrier_semaphore(), chips + 3)

    def to_sibling(k):
        c = lax.rem(chip + k, chips)
        return remote(x_ref.at[2 * c + 1 - core], came.at[c], s1.at[c], r1.at[c], (sibling, m))

    def to_chip(k):
        c = lax.rem(chip + k, chips)
        return remote(half.at[c], slots.at[chip], s2.at[c], r2.at[chip], (2 * c + core, m))

    def from_chip(k):
        c = lax.rem(chip + k, chips)
        return remote(half.at[c], slots.at[c], s2.at[c], r2.at[c], (2 * c + core, m))

    order = list(range(1, chips)) + [0]
    for k in order:
        to_sibling(k).start()
    for k in order:
        c = lax.rem(chip + k, chips)
        to_sibling(k).wait_recv()
        half[c] = pair_sum(x_ref[2 * c + core], came[c])
        if k:
            to_chip(k).start()
    mine[...] = half[chip].astype(f32)
    for k in range(1, chips):
        from_chip(k).wait_recv()
        mine[...] += slots[lax.rem(chip + k, chips)].astype(f32)
    cols = o_ref.shape[1]
    width = z_ref.shape[2]
    o_ref[...] = mine[:, :cols]
    for j in range(4):
        for t in range(2):
            at = cols + t * 4 * width + j * width
            blocks[j, t] = mine[:, at : at + width].astype(bf16)

    def to_plane(k):
        t = lax.rem(m + k, 4)
        return remote(blocks.at[t], blocks.at[4 + m], s3.at[k], r3.at[m], (d, t))

    for k in (1, 2, 3):
        to_plane(k).start()
    total = blocks[m].astype(f32)
    for k in (1, 2, 3):
        o = lax.rem(m + k, 4)
        remote(blocks.at[o], blocks.at[4 + o], s3.at[k], r3.at[o], (d, o)).wait_recv()
        total = total + blocks[4 + o].astype(f32)
    z_ref[...] = total
    for k in order:
        to_sibling(k).wait_send()
    for k in range(1, chips):
        to_chip(k).wait_send()
    for k in (1, 2, 3):
        to_plane(k).wait_send()


def scatter(x, width):
    n, rows, cols = x.shape
    kept = cols - 8 * width
    chips = n // 2
    dma = pltpu.SemaphoreType.DMA
    buffer = pltpu.VMEM((chips, rows, cols), bf16)
    return pl.pallas_call(
        functools.partial(scatter_kernel, n),
        out_shape=(jax.ShapeDtypeStruct((rows, kept), f32), jax.ShapeDtypeStruct((2, rows, width), f32)),
        in_specs=[VMEM],
        out_specs=[VMEM, VMEM],
        scratch_shapes=[
            buffer, buffer, buffer, pltpu.VMEM((rows, cols), f32), pltpu.VMEM((8, 2, rows, width), bf16),
            dma((chips,)), dma((chips,)), dma((chips,)), dma((chips,)), dma((4,)), dma((4,)),
        ],
        compiler_params=pltpu.CompilerParams(
            collective_id=4, has_side_effects=True, vmem_limit_bytes=56 * 2**20
        ),
        name="scatter",
    )(x)


def vectors_kernel(steps, x_ref, y_ref, ox_ref, oy_ref, xs, ys, xr, yr, s1, r1, s2, r2):
    d, m = lax.axis_index("dp"), lax.axis_index("mp")
    partners = [(flip(d, 1 << i), m) for i in range(steps)] + [(d, flip(m, 1)), (d, flip(m, 2))]
    greet(partners)
    pl.semaphore_wait(pltpu.get_barrier_semaphore(), steps + 2)
    xs[0] = x_ref[...]
    ys[0] = y_ref[...]
    for i in range(steps + 2):
        copies = [remote(ys.at[i], yr.at[i], s2.at[i], r2.at[i], partners[i])]
        if i < steps:
            copies.append(remote(xs.at[i], xr.at[i], s1.at[i], r1.at[i], partners[i]))
        for copy in copies:
            copy.start()
        for copy in copies:
            copy.wait()
        ys[i + 1] = ys[i] + yr[i]
        if i < steps:
            xs[i + 1] = xs[i] + xr[i]
    ox_ref[...] = xs[steps]
    oy_ref[...] = ys[steps + 2]


def vectors(x, y, n):
    steps = n.bit_length() - 1
    dma = pltpu.SemaphoreType.DMA
    return pl.pallas_call(
        functools.partial(vectors_kernel, steps),
        out_shape=(jax.ShapeDtypeStruct(x.shape, f32), jax.ShapeDtypeStruct(y.shape, f32)),
        in_specs=[VMEM, VMEM],
        out_specs=[VMEM, VMEM],
        scratch_shapes=[
            pltpu.VMEM((steps + 1,) + x.shape, f32), pltpu.VMEM((steps + 3,) + y.shape, f32),
            pltpu.VMEM((steps,) + x.shape, f32), pltpu.VMEM((steps + 2,) + y.shape, f32),
            dma((steps,)), dma((steps,)), dma((steps + 2,)), dma((steps + 2,)),
        ],
        compiler_params=pltpu.CompilerParams(collective_id=5, has_side_effects=True),
        name="vectors",
    )(x, y)


def layer_norm(values, norm_gain, offset):
    average = jnp.mean(values, axis=-1, keepdims=True)
    centred = values - average
    variance = jnp.mean(centred * centred, axis=-1, keepdims=True)
    return centred * lax.rsqrt(variance + epsilon) * norm_gain + offset


def exact_gelu(values):
    return jax.nn.gelu(values, approximate=False)


def product(left_side, right_side):
    return jnp.dot(left_side, right_side, preferred_element_type=f32)


def left_product(left_side, right_side):
    return lax.dot_general(left_side, right_side, (((0,), (0,)), ((), ())), preferred_element_type=f32)


def right_product(left_side, right_side):
    return lax.dot_general(left_side, right_side, (((1,), (1,)), ((), ())), preferred_element_type=f32)


def split_heads(matrix):
    return matrix.reshape(matrix.shape[0], -1, HEAD_DIM).transpose(1, 0, 2)


def merge_heads(stacked):
    return stacked.transpose(1, 0, 2).reshape(stacked.shape[1], -1)


def einsum(spec, a, b):
    return jnp.einsum(spec, a, b, preferred_element_type=f32)


def scores_of(q, k, allowed):
    return jnp.where(allowed, factor * einsum("htd,hsd->hts", q, k), masked_value)


def attention_forward(queries, key_rows, value_rows, allowed):
    q, k, v = split_heads(queries), split_heads(key_rows), split_heads(value_rows)
    scores = scores_of(q, k, allowed)
    row_max = jnp.max(scores, axis=-1, keepdims=True)
    exponent = jnp.exp(scores - row_max)
    row_total = jnp.sum(exponent, axis=-1, keepdims=True)
    probabilities = (exponent / row_total).astype(bf16)
    return einsum("hts,hsd->htd", probabilities, v), (row_max + jnp.log(row_total))[..., 0]


def attention_backward(queries, key_rows, value_rows, allowed, log_totals, upstream, inner=None):
    q, k, v, up = split_heads(queries), split_heads(key_rows), split_heads(value_rows), split_heads(upstream)
    p = jnp.exp(scores_of(q, k, allowed) - log_totals[..., None])
    value_grad = einsum("hts,htd->hsd", p.astype(bf16), up)
    prob_grad = einsum("htd,hsd->hts", up, v)
    if inner is None:
        inner = jnp.sum(p * prob_grad, axis=-1)
    score_grad = (p * (prob_grad - inner[..., None])).astype(bf16)
    return (
        merge_heads(factor * einsum("hts,hsd->htd", score_grad, k)),
        merge_heads(factor * einsum("hts,htd->hsd", score_grad, q)),
        merge_heads(value_grad),
    )


def by_owner(grad, n):
    return grad.astype(bf16).reshape(n, grad.shape[0] // n, grad.shape[1])


def shards(
    n, tokens, encoder, lengths, norm_gains, norm_biases, self_in, cross_in, in_biases, self_out, cross_out,
    out_biases, fc_up, up_bias, fc_down, cotangent,
):
    row_count, width = tokens.shape
    clip_count, frame_count = encoder.shape[:2]
    own = self_in.shape[2]
    mp = lax.axis_index("mp")
    positions = jnp.arange(row_count, dtype=jnp.int32)
    clip_ends = jnp.cumsum(lengths[0])
    token_clip = jnp.sum((positions[:, None] >= clip_ends[None, :]).astype(jnp.int32), axis=1)
    self_allowed = (token_clip[:, None] == token_clip[None, :]) & (positions[None, :] <= positions[:, None])
    frames = encoder.reshape(clip_count * frame_count, -1)
    frame_clip = jnp.arange(clip_count * frame_count, dtype=jnp.int32) // frame_count
    cross_allowed = token_clip[:, None] == frame_clip[None, :]

    inputs = tokens.astype(f32)
    normed_self, pull_first = jax.vjp(layer_norm, inputs, norm_gains[0], norm_biases[0])
    normed_self = normed_self.astype(bf16)
    self_queries = (product(normed_self, self_in[0]) + in_biases[0]).astype(bf16)
    self_keys = product(normed_self, self_in[1]).astype(bf16)
    self_values = (product(normed_self, self_in[2]) + in_biases[1]).astype(bf16)
    attended, self_totals = attention_forward(self_queries, self_keys, self_values, self_allowed)
    self_attended = merge_heads(attended).astype(bf16)

    pack = jnp.concatenate(
        [self_out, cross_in[0].T, cross_in[1].T, cross_in[2].T, cross_out, jnp.zeros((64, width), bf16)]
    ).reshape(PLANE, -1, width)
    halves = row_count // 2
    sent = jnp.concatenate([self_attended[:halves], self_attended[halves:]], axis=1)
    weights, parts = gather(pack, sent)
    weights = weights.reshape(4, -1, width)[:, : 5 * own].reshape(4, 5, own, width)
    weights = weights.transpose(1, 0, 2, 3).reshape(5, 4 * own, width)
    whole_self_out, query_in, key_in, value_in, whole_cross_out = weights
    parts = parts.reshape(4, halves, 2, own).transpose(2, 1, 0, 3).reshape(row_count, 4 * own)

    middle = inputs + product(parts, whole_self_out) + out_biases[0]
    normed_cross, pull_second = jax.vjp(layer_norm, middle, norm_gains[1], norm_biases[1])
    normed_cross = normed_cross.astype(bf16)
    biases = share(in_biases[2:].reshape(2, own), 3).transpose(1, 0, 2).reshape(2, 4 * own)
    cross_queries = (right_product(normed_cross, query_in) + biases[0]).astype(bf16)
    cross_keys = right_product(frames, key_in).astype(bf16)
    cross_values = (right_product(frames, value_in) + biases[1]).astype(bf16)
    local_out, local_totals = attention_forward(cross_queries, cross_keys, cross_values, cross_allowed)
    all_totals = share(jnp.pad(local_totals, ((0, 4), (0, 0))), 6)[:, :12]
    top = jnp.max(all_totals, axis=0)
    cross_totals = top + jnp.log(jnp.sum(jnp.exp(all_totals - top), axis=0))
    local_out = local_out * jnp.exp(local_totals - cross_totals)[..., None]
    cross_attended = total(merge_heads(local_out).astype(bf16))
    after_cross = middle + product(cross_attended, whole_cross_out) + out_biases[1]

    normed_mlp, pull_third = jax.vjp(layer_norm, after_cross, norm_gains[2], norm_biases[2])
    normed_mlp = normed_mlp.astype(bf16)
    upward = product(normed_mlp, fc_up) + up_bias
    active, pull_gelu = jax.vjp(exact_gelu, upward)
    active = active.astype(bf16)
    down = total(product(active, fc_down).astype(bf16))
    layer_out = (after_cross + down.astype(f32) + out_biases[2]).astype(bf16)

    grad_low = cotangent
    grad_out = cotangent.astype(f32)
    down_bias_grad = jnp.sum(grad_out, axis=0)
    fc_down_grad = left_product(grad_low, active)
    (upward_grad,) = pull_gelu(right_product(grad_low, fc_down))
    up_bias_grad = jnp.sum(upward_grad, axis=0)
    upward_low = upward_grad.astype(bf16)
    fc_up_grad = left_product(normed_mlp, upward_low)
    mlp_normed_grad = total(right_product(upward_low, fc_up).astype(bf16)).astype(f32)
    cross_side_grad, third_gain_grad, third_bias_grad = pull_third(mlp_normed_grad)
    cross_side_grad = cross_side_grad + grad_out
    cross_bias_grad = jnp.sum(cross_side_grad, axis=0)
    cross_side_low = cross_side_grad.astype(bf16)
    own_cols = lambda a: lax.dynamic_slice_in_dim(a, mp * own, own, axis=1)
    cross_out_grad = left_product(cross_side_low, own_cols(cross_attended))
    cross_upstream = right_product(cross_side_low, whole_cross_out).astype(bf16)
    inner = jnp.sum(split_heads(cross_upstream).astype(f32) * split_heads(cross_attended).astype(f32), axis=-1)
    query_grad, key_grad, value_grad = attention_backward(
        cross_queries, cross_keys, cross_values, cross_allowed, cross_totals, cross_upstream, inner
    )
    cross_query_low = total(query_grad.astype(bf16))
    cross_value_bias = jnp.sum(value_grad, axis=0)
    cross_query_bias = jnp.sum(own_cols(cross_query_low).astype(f32), axis=0)
    key_low, value_low = key_grad.astype(bf16), value_grad.astype(bf16)
    query_weight_grad = left_product(normed_cross, own_cols(cross_query_low))
    key_weight_grad = left_product(frames, key_low)
    value_weight_grad = left_product(frames, value_low)
    encoder_grad = (product(key_low, key_in) + product(value_low, value_in)).astype(bf16)
    encoder_grad = encoder_grad.reshape(clip_count, frame_count, -1)
    cross_normed_grad = product(cross_query_low, query_in)
    middle_grad, second_gain_grad, second_bias_grad = pull_second(cross_normed_grad)
    middle_grad = middle_grad + cross_side_grad
    self_bias_grad = jnp.sum(middle_grad, axis=0)
    middle_low = middle_grad.astype(bf16)
    self_out_grad = left_product(middle_low, self_attended)
    self_upstream = right_product(middle_low, self_out).astype(bf16)
    query_grad, key_grad, value_grad = attention_backward(
        self_queries, self_keys, self_values, self_allowed, self_totals, self_upstream
    )
    self_query_bias = jnp.sum(query_grad, axis=0)
    self_value_bias = jnp.sum(value_grad, axis=0)
    lows = [query_grad.astype(bf16), key_grad.astype(bf16), value_grad.astype(bf16)]
    self_in_grad = [left_product(normed_self, low) for low in lows]
    self_term = sum(right_product(low, self_in[i]) for i, low in enumerate(lows))
    self_normed_grad = total(self_term.astype(bf16)).astype(f32)
    input_grad, first_gain_grad, first_bias_grad = pull_first(self_normed_grad)
    token_grad = (input_grad + middle_grad).astype(bf16)

    grads = self_in_grad + [
        query_weight_grad, fc_up_grad, fc_down_grad, self_out_grad, cross_out_grad, key_weight_grad,
        value_weight_grad,
    ]
    kept, shared = scatter(jnp.concatenate([by_owner(g, n) for g in grads], axis=2), own)
    hidden = fc_up.shape[1]
    pieces = jnp.split(
        kept, [own, 2 * own, 3 * own, 4 * own, 4 * own + hidden, 4 * own + 2 * hidden, 5 * own + 2 * hidden], axis=1
    )
    self_in_grad = jnp.stack(pieces[:3])
    cross_in_grad = jnp.stack([pieces[3], shared[0], shared[1]])
    fc_up_grad, fc_down_grad, self_out_grad, cross_out_grad = (
        pieces[4], pieces[5].T, pieces[6].T, pieces[7].T,
    )
    pad = lambda v: jnp.pad(v, (0, width - v.shape[0]))
    rows = [
        first_gain_grad, second_gain_grad, third_gain_grad, first_bias_grad, second_bias_grad, third_bias_grad,
        self_bias_grad, cross_bias_grad, down_bias_grad, pad(self_query_bias), pad(self_value_bias),
        pad(cross_query_bias),
    ]
    rows = rows + list(up_bias_grad.reshape(-1, width))
    rows = rows + [jnp.zeros((width,), f32)] * (-len(rows) % 8)
    extra = jnp.pad(cross_value_bias[None], ((0, 7), (0, 0)))
    sums, extra = vectors(jnp.stack(rows), extra, n)
    in_biases_grad = jnp.stack(
        [sums[9, :own], sums[10, :own], sums[11, :own], lax.dynamic_slice_in_dim(extra[0], mp * own, own)]
    )
    return (
        layer_out, token_grad, encoder_grad, sums[0:3], sums[3:6], self_in_grad, cross_in_grad, in_biases_grad,
        self_out_grad, cross_out_grad, sums[6:9], fc_up_grad, sums[12 : 12 + hidden // width].reshape(hidden),
        fc_down_grad,
    )


def solution(mesh):
    in_specs = (
        P("dp", None), P("dp", "mp", None), P("dp", None), P(), P(), P(None, None, "mp"), P(None, None, "mp"),
        P(None, "mp"), P("mp", None), P("mp", None), P(), P(None, "mp"), P("mp"), P("mp", None), P("dp", None),
    )
    out_specs = (
        P("dp", None), P("dp", None), P("dp", "mp", None), P(), P(), P(None, "dp", "mp"), P(None, "dp", "mp"),
        P(None, "mp"), P("mp", "dp"), P("mp", "dp"), P(), P("dp", "mp"), P("mp"), P("mp", "dp"),
    )
    body = functools.partial(shards, mesh.shape["dp"])
    return jax.shard_map(body, mesh=mesh, in_specs=in_specs, out_specs=out_specs, check_vma=False)
```

time: 1130 us -> 522 us (0.46)
  blocking collectives: 436 us -> 0 us
  waiting for transfers between devices: 341 us -> 0 us
  Pallas kernels: 0 us -> 277 us
  local copies, waits for them, and re-layouts: 130 us -> 76.6 us
  matrix products: 140 us -> 118 us
  other arithmetic: 53.6 us -> 37.5 us
  between operations: 16.2 us -> 2.41 us
    unnamed x1 -> x0, blocking collectives: 412 us -> none
    pallas_call x0 -> x10, Pallas kernels: none -> 277 us  [the longest x5 132 us: total(): pl.pallas_call(functools.partial(total_kernel, count, lag), out_shape=jax...]
    psum x5 -> x0, waiting for transfers between devices: 256 us -> none  [the longest x1 70.5 us: shards(): lax.psum(product(self_attended, self_out), 'mp')]
    all_gather x1 -> x0, waiting for transfers between devices: 83.6 us -> none  [shards(): frame_piece = lax.all_gather(encoder, 'mp', axis=1, tiled=True)]
    reshape x9 -> x3, local copies, waits for them, and re-layouts: 45.8 us -> 4.39 us  [the longest x1 2.52 us: shards(): encoder_grad = encoder_grad.reshape(clip_count, frame_count, -1)]
    dot_general x28 -> x10, matrix products: 60.8 us -> 21.4 us  [right_product(): lax.dot_general(left_side, right_side, (((1,), (1,)), ((), ())), preferre...]
    dot_general x22, matrix products: 40.5 us -> 77.2 us  [the longest x12 59 us: einsum(): return jnp.einsum(spec, a, b, preferred_element_type=f32)]
    unnamed x211 -> x222, local copies, waits for them, and re-layouts: 43.5 us -> 17.1 us
  transfers between devices with their start and end apart: 12 -> 0, of which waited for: 5 -> 0; matrix products, arithmetic and copies ran while one was open for 16% -> 0% of each run, Pallas kernels for 0% -> 0%
where the time goes in v1:
time: 522 us; the launch traced here: 511 us
  Pallas kernels  277 us (53%)
  matrix products  118 us (23%)
  local copies, waits for them, and re-layouts  76.6 us (15%)
  other arithmetic  37.5 us (7%)
    pallas_call x5, Pallas kernels, total(): pl.pallas_call(functools.partial(total_kernel, count, lag), out_shape=jax...  132 us
    dot_general x12, matrix products, einsum(): return jnp.einsum(spec, a, b, preferred_element_type=f32)  59 us
    pallas_call x1, Pallas kernels, gather(): pl.pallas_call(gather_kernel, out_shape=(jax.ShapeDtypeStruct((4,) + pack...  58.5 us
    pallas_call x1, Pallas kernels, scatter(): pl.pallas_call(functools.partial(scatter_kernel, n), out_shape=(jax.Shape...  51.2 us
    dot_general x10, matrix products, right_product(): lax.dot_general(left_side, right_side, (((1,), (1,)), ((), ())), preferre...  21.4 us
    dot_general x10, matrix products, left_product(): lax.dot_general(left_side, right_side, (((0,), (0,)), ((), ())), preferre...  19.3 us
    pallas_call x1, Pallas kernels, vectors(): pl.pallas_call(functools.partial(vectors_kernel, steps), out_shape=(jax.S...  18.8 us
    dot_general x10, matrix products, product(): return jnp.dot(left_side, right_side, preferred_element_type=f32)  18.3 us

profile of v1, /device:TPU:0, one launch (start us, length us, event | category | flops | bytes accessed | tf_op | source)
XLA Modules:
  0.0 511.5 jit_solution(7001289733396738472)
XLA Ops:
  6.0 8.6 %share.2 = f32[4,2,192]{2,1,0:T(2,128)} custom-call(f32[2,192]{1,0:T(2,128)} %slice.130.x_ref), custom_call_target="tpu_custom_call" | custom-call | tf_op jit(solution)/shard_map/share/pallas_call | solution.py:284
  33.1 58.5 %gather.1 = (bf16[4,8,128,768]{3,2,1,0:T(8,128)(2,1)}, bf16[4,256,384]{2,1,0:T(8,128)(2,1)}, f32[8,128]{1,0:T(8,128)}) custom-call(bf16[8,128,768]{2,1,0:T(8,128)(2,1)} %bitcast.221, bf16[256,384]{1,0:T(8,128)(2,1)} %pad_maximum_fusion.2.attended), custom_call_target="tpu_custom_call" | custom-call | tf_op jit(solution)/shard_map/gather/pallas_call | solution.py:175
  94.0 3.1 slice.146
  97.1 1.9 fusion.89
  101.5 1.7 add_convert_fusion.6
  103.2 2.4 copy.81
  105.6 3.4 fusion.36
  109.0 2.7 copy.84
  111.6 3.4 fusion.37
  116.6 9.6 %fusion.2 = (f32[12,512]{1,0:T(8,128)S(1)}, f32[12,512,750]{1,2,0:T(8,128)}) fusion(pred[512,750]{0,1:T(8,128)(4,1)S(1)} %broadcast_compare_fusion, bf16[12,512,64]{1,2,0:T(8,128)(2,1)} %bitcast.214, bf16[12,750,64]{1,2,0:T(8,128)(2,1)S(1)} %bitcast.212), kind=kOutput, calls=%fused_computation.7 | convolution fusion | flops 603641856 | bytes 20779008 | tf_op jit(solution)/shard_map/htd,hsd->hts/dot_general | solution.py:456
  126.2 10.1 %fusion = f32[12,512]{1,0:T(8,128)S(1)} fusion(f32[12,512,750]{1,2,0:T(8,128)} %get-tuple-element.132, f32[12,512]{1,0:T(8,128)S(1)} %get-tuple-element.131, pred[512,750]{0,1:T(8,128)(4,1)S(1)} %broadcast_compare_fusion), kind=kLoop, calls=%fused_computation.5 | loop fusion | flops 18425856 | bytes 18865152 | tf_op jit(solution)/shard_map/reduce_sum | solution.py:468
  137.0 7.9 %share.3 = f32[4,16,512]{2,1,0:T(8,128)} custom-call(f32[16,512]{1,0:T(8,128)} %pad.18.x_ref), custom_call_target="tpu_custom_call" | custom-call | tf_op jit(solution)/shard_map/share/pallas_call | solution.py:284
  147.4 10.0 %fusion.28 = bf16[512,12,64]{0,2,1:T(8,128)(2,1)} fusion(bf16[12,750,64]{1,2,0:T(8,128)(2,1)S(1)} %bitcast.249, f32[12,512,750]{1,2,0:T(8,128)} %get-tuple-element.132, f32[12,512]{1,0:T(8,128)S(1)} %fusion, f32[12,512]{1,0:T(8,128)S(1)} %get-tuple-element.131, pred[512,750]{0,1:T(8,128)(4,1)S(1)} %broadcast_compare_fusion, f32[512,12]{0,1:T(8,128)S(1)} %get-tuple-element.99), kind=kOutput, calls=%fused_computation.58 | convolution fusion | flops 613650432 | bytes 20828160 | tf_op jit(solution)/shard_map/hts,hsd->htd/dot_general | solution.py:456
  157.4 2.3 copy.85.x_ref
  159.7 28.4 %total.5 = bf16[512,768]{1,0:T(8,128)(2,1)} custom-call(bf16[512,768]{1,0:T(8,128)(2,1)} %copy.85.x_ref), custom_call_target="tpu_custom_call" | custom-call | tf_op jit(solution)/shard_map/total/pallas_call | solution.py:257
  188.1 2.9 fusion.97
  192.5 2.1 convolution_add_fusion
  196.1 6.4 %fusion.84 = (f32[768]{0:T(1024)S(1)}, bf16[512,768]{1,0:T(8,128)(2,1)}, f32[512,768]{1,0:T(8,128)S(1)}) fusion(f32[512,768]{1,0:T(8,128)} %convolution_add_fusion, bf16[512,768]{1,0:T(8,128)(2,1)} %param.29, bf16[768,768]{1,0:T(8,128)(2,1)S(1)} %copy-done), kind=kOutput, calls=%fused_computation.213 | convolution fusion | flops 632683776 | bytes 5901312 | tf_op jit(solution)/shard_map/dot_general | solution.py:444
  205.2 25.2 %total.6 = bf16[512,768]{1,0:T(8,128)(2,1)} custom-call(bf16[512,768]{1,0:T(8,128)(2,1)} %convolution_convert_fusion.7.x_ref), custom_call_target="tpu_custom_call" | custom-call | tf_op jit(solution)/shard_map/total/pallas_call | solution.py:257
  230.5 3.1 convolution_convert_fusion.2
  233.7 1.7 convolution_convert_fusion.6.x_ref
  235.3 23.1 %total.7 = bf16[512,768]{1,0:T(8,128)(2,1)} custom-call(bf16[512,768]{1,0:T(8,128)(2,1)} %convolution_convert_fusion.6.x_ref), custom_call_target="tpu_custom_call" | custom-call | tf_op jit(solution)/shard_map/total/pallas_call | solution.py:257
  258.5 1.7 convert_reduce_fusion.1
  262.3 2.0 convolution_convert_fusion.3
  264.4 2.3 fusion.86
  272.2 10.1 %bitcast_reduce_fusion = (f32[12,64]{1,0:T(8,128)S(1)}, bf16[12,750,64]{1,2,0:T(8,128)(2,1)}) fusion(bf16[12,512,64]{1,2,0:T(8,128)(2,1)S(1)} %bitcast.219, f32[12,512,750]{1,2,0:T(8,128)} %get-tuple-element.132, f32[12,512]{1,0:T(8,128)S(1)} %copy-done.68, pred[512,750]{0,1:T(8,128)(4,1)S(1)} %copy-done.19), kind=kOutput, calls=%fused_computation.36 | convolution fusion | flops 609407232 | bytes 20782080 | tf_op jit(solution)/shard_map/hts,htd->hsd/dot_general | solution.py:456
  282.3 11.8 %multiply_convert_fusion = bf16[12,512,750]{1,2,0:T(8,128)(2,1)} fusion(f32[12,512,750]{1,2,0:T(8,128)} %get-tuple-element.132, f32[12,512]{1,0:T(8,128)S(1)} %multiply_reduce_fusion.3, f32[12,512]{1,0:T(8,128)S(1)} %copy-done.68, pred[512,750]{0,1:T(8,128)(4,1)S(1)} %copy-done.19, bf16[12,512,64]{1,2,0:T(8,128)(2,1)S(1)} %bitcast.220, ...), kind=kOutput, calls=%fused_computation | convolution fusion | flops 617472000 | bytes 30019584 | tf_op jit(solution)/shard_map/htd,hsd->hts/dot_general | solution.py:456
  294.1 5.4 %multiply_convert_fusion.3 = bf16[12,512,64]{1,2,0:T(8,128)(2,1)S(1)} fusion(bf16[12,512,750]{1,2,0:T(8,128)(2,1)} %multiply_convert_fusion, bf16[12,750,64]{1,2,0:T(8,128)(2,1)S(1)} %bitcast.213), kind=kOutput, calls=%fused_computation.64 | convolution fusion | flops 590610432 | bytes 11154432 | tf_op jit(solution)/shard_map/hts,hsd->htd/dot_general | solution.py:456
  299.6 7.5 %multiply_convert_fusion.2 = bf16[12,750,64]{1,2,0:T(8,128)(2,1)} fusion(bf16[12,512,750]{1,2,0:T(8,128)(2,1)} %multiply_convert_fusion, bf16[12,512,64]{1,2,0:T(8,128)(2,1)S(1)} %bitcast.215), kind=kOutput, calls=%fused_computation.38 | convolution fusion | flops 590976000 | bytes 11154432 | tf_op jit(solution)/shard_map/hts,htd->hsd/dot_general | solution.py:456
  308.3 23.4 %total.8 = bf16[512,768]{1,0:T(8,128)(2,1)} custom-call(bf16[512,768]{1,0:T(8,128)(2,1)} %copy.88.x_ref), custom_call_target="tpu_custom_call" | custom-call | tf_op jit(solution)/shard_map/total/pallas_call | solution.py:257
  334.6 2.3 multiply_reduce_fusion.1
  342.7 2.4 convolution_convert_fusion.8
  345.1 2.0 copy.96
  348.1 1.8 convolution_convert_fusion.14
  353.8 2.2 convolution_convert_fusion.9
  356.0 1.9 copy.94
  357.9 2.9 fusion.98
  360.8 2.2 add_convert_fusion
  363.0 2.2 convolution_convert_fusion
  365.2 2.2 convolution_convert_fusion.1
  367.4 2.5 reshape.359
  369.9 3.2 copy.98
  380.9 10.8 %concatenate.11.x_ref = bf16[8,96,4224]{2,1,0:T(8,128)(2,1)} concatenate(bf16[8,96,192]{2,1,0:T(8,128)(2,1)S(1)} %bitcast.235, bf16[8,96,192]{2,1,0:T(8,128)(2,1)S(1)} %bitcast.234, bf16[8,96,192]{2,1,0:T(8,128)(2,1)S(1)} %bitcast.233, bf16[8,96,192]{2,1,0:T(8,128)(2,1)S(1)} %bitcast.232, bf16[8,96,768]{2,1,0:T(8,128)(2,1)} %bitcast.241, bf16[8,96,768]{2,1,0:T(8,128)(2,1)} %bitcast.240, ...), dimensions={2} | concatenate | bytes 12976128 | tf_op jit(solution)/shard_map/concatenate | solution.py:603
  391.7 51.2 %scatter.1 = (f32[96,2688]{1,0:T(8,128)}, f32[2,96,192]{2,1,0:T(8,128)}) custom-call(bf16[8,96,4224]{2,1,0:T(8,128)(2,1)} %concatenate.11.x_ref), custom_call_target="tpu_custom_call" | custom-call | tf_op jit(solution)/shard_map/scatter/pallas_call | solution.py:368
  450.4 31.9 %total.9 = bf16[512,768]{1,0:T(8,128)(2,1)} custom-call(bf16[512,768]{1,0:T(8,128)(2,1)} %add_convert_fusion.3.x_ref), custom_call_target="tpu_custom_call" | custom-call | tf_op jit(solution)/shard_map/total/pallas_call | solution.py:257
  482.4 1.7 convert_reduce_fusion
  486.6 18.8 %vectors.1 = (f32[16,768]{1,0:T(8,128)}, f32[8,768]{1,0:T(8,128)}) custom-call(f32[16,768]{1,0:T(8,128)} %stack.61.x_ref, f32[8,768]{1,0:T(8,128)} %pad.22.y_ref), custom_call_target="tpu_custom_call" | custom-call | tf_op jit(solution)/shard_map/vectors/pallas_call | solution.py:409
  506.2 3.0 add_convert_fusion.2
  (334 shorter events, 80.9 us)
Async XLA Ops:
  0.6 195.4 %copy-start = (bf16[768,768]{1,0:T(8,128)(2,1)S(1)}, bf16[768,768]{1,0:T(8,128)(2,1)}, u32[]{:S(2)}) copy-start(bf16[768,768]{1,0:T(8,128)(2,1)} %param.28) | copy-start | bytes 3538948
  0.7 17.9 %copy-start.4 = (bf16[512,768]{1,0:T(8,128)(2,1)S(1)}, bf16[512,768]{1,0:T(8,128)(2,1)}, u32[]{:S(2)}) copy-start(bf16[512,768]{1,0:T(8,128)(2,1)} %param.15) | copy-start | bytes 2359300
  0.7 5.3 %copy-start.93 = (f32[4,192]{1,0:T(4,128)S(1)}, f32[4,192]{1,0:T(4,128)}, u32[]{:S(2)}) copy-start(f32[4,192]{1,0:T(4,128)} %param.22) | copy-start | bytes 9220
  0.7 15.5 %copy-start.90 = (f32[3,768]{1,0:T(4,128)S(1)}, f32[3,768]{1,0:T(4,128)}, u32[]{:S(2)}) copy-start(f32[3,768]{1,0:T(4,128)} %param.25) | copy-start | bytes 27652
  0.7 16.1 %copy-start.91 = (f32[3,768]{1,0:T(4,128)S(1)}, f32[3,768]{1,0:T(4,128)}, u32[]{:S(2)}) copy-start(f32[3,768]{1,0:T(4,128)} %param.19) | copy-start | bytes 27652
  0.7 16.1 %copy-start.92 = (f32[3,768]{1,0:T(4,128)S(1)}, f32[3,768]{1,0:T(4,128)}, u32[]{:S(2)}) copy-start(f32[3,768]{1,0:T(4,128)} %param.18) | copy-start | bytes 27652
  4.4 14.6 %copy-start.59 = (f32[512]{0:T(512)}, f32[512]{0:T(512)S(1)}, u32[]{:S(2)}) copy-start(f32[512]{0:T(512)S(1)} %broadcast_multiply_fusion.2) | copy-start | bytes 6148
  4.4 14.6 %copy-start.43 = (bf16[3,768,192]{1,2,0:T(8,128)(2,1)S(1)}, bf16[3,768,192]{1,2,0:T(8,128)(2,1)}, u32[]{:S(2)}) copy-start(bf16[3,768,192]{1,2,0:T(8,128)(2,1)} %param.20) | copy-start | bytes 2654212
  5.9 10.8 %copy-start.73 = (f32[512]{0:T(512)}, f32[512]{0:T(512)S(1)}, u32[]{:S(2)}) copy-start(f32[512]{0:T(512)S(1)} %fusion.20) | copy-start | bytes 6148
  6.0 14.1 %copy-start.64 = (f32[512]{0:T(512)}, f32[512]{0:T(512)S(1)}, u32[]{:S(2)}) copy-start(f32[512]{0:T(512)S(1)} %fusion.74) | copy-start | bytes 6148
  17.4 82.9 %copy-start.62 = (f32[768]{0:T(1024)}, f32[768]{0:T(1024)S(1)}, u32[]{:S(2)}) copy-start(f32[768]{0:T(1024)S(1)} %get-tuple-element.142) | copy-start | bytes 9220
  18.6 128.8 %copy-start.18 = (pred[512,750]{0,1:T(8,128)(4,1)}, pred[512,750]{0,1:T(8,128)(4,1)S(1)}, u32[]{:S(2)}) copy-start(pred[512,750]{0,1:T(8,128)(4,1)S(1)} %broadcast_compare_fusion) | copy-start | bytes 1152004
  23.7 4.0 copy-start.53
  23.7 5.2 %copy-start.42 = (pred[512,512]{0,1:T(8,128)(4,1)S(1)}, pred[512,512]{0,1:T(8,128)(4,1)}, u32[]{:S(2)}) copy-start(pred[512,512]{0,1:T(8,128)(4,1)} %fusion.46) | copy-start | bytes 786436
  23.7 5.2 %copy-start.47 = (bf16[512,192]{0,1:T(8,128)(2,1)S(1)}, bf16[512,192]{0,1:T(8,128)(2,1)}, u32[]{:S(2)}) copy-start(bf16[512,192]{0,1:T(8,128)(2,1)} %convolution_convert_fusion.15) | copy-start | bytes 589828
  23.7 5.2 %copy-start.51 = (bf16[512,192]{0,1:T(8,128)(2,1)S(1)}, bf16[512,192]{0,1:T(8,128)(2,1)}, u32[]{:S(2)}) copy-start(bf16[512,192]{0,1:T(8,128)(2,1)} %fusion.43) | copy-start | bytes 589828
  32.1 59.5 %copy-start.49 = (bf16[3,512,64]{1,2,0:T(8,128)(2,1)}, bf16[3,512,64]{1,2,0:T(8,128)(2,1)S(1)}, u32[]{:S(2)}) copy-start(bf16[3,512,64]{1,2,0:T(8,128)(2,1)S(1)} %fusion.45) | copy-start | bytes 589828
  116.6 9.6 %copy-start.15 = (bf16[750,768]{0,1:T(8,128)(2,1)}, bf16[750,768]{0,1:T(8,128)(2,1)S(1)}, u32[]{:S(2)}) copy-start(bf16[750,768]{0,1:T(8,128)(2,1)S(1)} %copy.83) | copy-start | bytes 3456004
  126.2 21.2 %copy-start.37 = (bf16[750,768]{0,1:T(8,128)(2,1)S(1)}, bf16[750,768]{0,1:T(8,128)(2,1)}, u32[]{:S(2)}) copy-start(bf16[750,768]{0,1:T(8,128)(2,1)} %copy.84) | copy-start | bytes 3456004
  157.4 30.7 %copy-start.95 = (f32[768]{0:T(1024)S(1)}, f32[768]{0:T(1024)}, u32[]{:S(2)}) copy-start(f32[768]{0:T(1024)} %get-tuple-element.81) | copy-start | bytes 9220
  196.1 6.4 %copy-start.30 = (f32[512,768]{1,0:T(8,128)S(1)}, f32[512,768]{1,0:T(8,128)}, u32[]{:S(2)}) copy-start(f32[512,768]{1,0:T(8,128)} %convolution_add_fusion) | copy-start | bytes 4718596
  205.2 25.2 %copy-start.45 = (bf16[512,768]{1,0:T(8,128)(2,1)S(1)}, bf16[512,768]{1,0:T(8,128)(2,1)}, u32[]{:S(2)}) copy-start(bf16[512,768]{1,0:T(8,128)(2,1)} %param.29) | copy-start | bytes 2359300
  230.5 3.2 copy-start.100
  230.5 3.2 copy-start.104
  272.2 10.1 %copy-start.38 = (bf16[750,768]{0,1:T(8,128)(2,1)S(1)}, bf16[750,768]{0,1:T(8,128)(2,1)}, u32[]{:S(2)}) copy-start(bf16[750,768]{0,1:T(8,128)(2,1)} %copy.84) | copy-start | bytes 3456004
  282.3 11.8 %copy-start.16 = (bf16[750,768]{0,1:T(8,128)(2,1)S(1)}, bf16[750,768]{0,1:T(8,128)(2,1)}, u32[]{:S(2)}) copy-start(bf16[750,768]{0,1:T(8,128)(2,1)} %copy-done.15) | copy-start | bytes 3456004
  294.1 5.4 %copy-start.20 = (bf16[512,768]{0,1:T(8,128)(2,1)S(1)}, bf16[512,768]{0,1:T(8,128)(2,1)}, u32[]{:S(2)}) copy-start(bf16[512,768]{0,1:T(8,128)(2,1)} %copy.81) | copy-start | bytes 2359300
  307.1 24.6 %copy-start.23 = (bf16[512,768]{1,0:T(8,128)(2,1)S(1)}, bf16[512,768]{1,0:T(8,128)(2,1)}, u32[]{:S(2)}) copy-start(bf16[512,768]{1,0:T(8,128)(2,1)} %copy-done.22) | copy-start | bytes 2359300
  308.3 26.3 %copy-start.7 = (f32[512,768]{1,0:T(8,128)S(1)}, f32[512,768]{1,0:T(8,128)}, u32[]{:S(2)}) copy-start(f32[512,768]{1,0:T(8,128)} %copy-done.6) | copy-start | bytes 4718596
  308.3 26.3 %copy-start.63 = (f32[768]{0:T(1024)S(1)}, f32[768]{0:T(1024)}, u32[]{:S(2)}) copy-start(f32[768]{0:T(1024)} %copy-done.62) | copy-start | bytes 9220
  308.3 26.3 %copy-start.67 = (f32[512]{0:T(512)S(1)}, f32[512]{0:T(512)}, u32[]{:S(2)}) copy-start(f32[512]{0:T(512)} %copy-done.66) | copy-start | bytes 6148
  308.3 26.3 %copy-start.70 = (f32[512]{0:T(512)S(1)}, f32[512]{0:T(512)}, u32[]{:S(2)}) copy-start(f32[512]{0:T(512)} %copy-done.69) | copy-start | bytes 6148
  338.9 3.7 copy-start.50
  345.1 4.8 copy-start.3
  369.9 3.2 copy-start.55
  377.5 3.3 copy-start.26
  377.5 3.3 copy-start.27
  377.5 3.3 copy-start.28
  377.5 3.3 copy-start.29
  442.9 3.9 copy-start.56
  444.5 3.8 copy-start.44
  450.4 31.9 %copy-start.5 = (bf16[512,768]{1,0:T(8,128)(2,1)S(1)}, bf16[512,768]{1,0:T(8,128)(2,1)}, u32[]{:S(2)}) copy-start(bf16[512,768]{1,0:T(8,128)(2,1)} %param.15) | copy-start | bytes 2359300
  450.4 31.9 %copy-start.58 = (f32[768]{0:T(1024)S(1)}, f32[768]{0:T(1024)}, u32[]{:S(2)}) copy-start(f32[768]{0:T(1024)} %copy-done.57) | copy-start | bytes 9220
  450.4 32.0 %copy-start.60 = (f32[512]{0:T(512)S(1)}, f32[512]{0:T(512)}, u32[]{:S(2)}) copy-start(f32[512]{0:T(512)} %copy-done.59) | copy-start | bytes 6148
  450.4 33.8 %copy-start.74 = (f32[512]{0:T(512)S(1)}, f32[512]{0:T(512)}, u32[]{:S(2)}) copy-start(f32[512]{0:T(512)} %copy-done.73) | copy-start | bytes 6148
  450.4 33.8 %copy-start.65 = (f32[512]{0:T(512)S(1)}, f32[512]{0:T(512)}, u32[]{:S(2)}) copy-start(f32[512]{0:T(512)} %copy-done.64) | copy-start | bytes 6148
  506.2 4.8 copy-start.1
  506.2 3.0 copy-start.61
  (58 other events, 116.2 us)
